TPU v7x, 512 devices: a whole 4x4x16 slice. The times are simulated.
512 devices in a mesh: dp: 8 (over x, core), expouter: 8 (over z_lo), expinner: 8 (over z_hi, y).
Axes of the slice: x: 4, y: 4, z: 16 (z_hi: 2, z_lo: 8; z = z_hi * 8 + z_lo), core: 2. Of those that a mesh axis runs over, the one named last changes fastest.
Arguments:
- tokens: bfloat16 [65536, 1024], P(('dp', 'expouter', 'expinner')), may hold values from -6 to 6
- cotangent: bfloat16 [65536, 1024], P(('dp', 'expouter', 'expinner')), may hold values from -6 to 6
- gate_probs: float32 [65536, 2], P(('dp', 'expouter', 'expinner')), may hold values from 0.05 to 1
- expert_ids: int32 [65536, 2], P(('dp', 'expouter', 'expinner')), may hold values from 0 to 63, all different within a row; in each aligned block of 128 rows (0 to 127, 128 to 255, ...) at most 5 rows name the same one
- gate_weight: bfloat16 [64, 1024, 768], P(('expouter', 'expinner'), 'dp'), may hold values from -0.1875 to 0.1875
- up_weight: bfloat16 [64, 1024, 768], P(('expouter', 'expinner'), 'dp'), may hold values from -0.1875 to 0.1875
- down_weight: bfloat16 [64, 1024, 768], P(('expouter', 'expinner'), 'dp'), may hold values from -0.21875 to 0.21875
Outputs:
- mixed: bfloat16 [65536, 1024], P(('dp', 'expouter', 'expinner'))
- grad_tokens: bfloat16 [65536, 1024], P(('dp', 'expouter', 'expinner'))
- grad_probs: float32 [65536, 2], P(('dp', 'expouter', 'expinner'))
- grad_gate: float32 [64, 1024, 768], P(('expouter', 'expinner'), 'dp')
- grad_up: float32 [64, 1024, 768], P(('expouter', 'expinner'), 'dp')
- grad_down: float32 [64, 1024, 768], P(('expouter', 'expinner'), 'dp')
Inputs may be any that keep to these rules, and one draw needn't show every extreme that they name: `expert_ids`: among the tokens of one device (aligned blocks of 128 tokens) no expert is named more than 5 times, a bound that some block reaches; a token's 2 experts differ.
All inputs are finite; a program needn't handle non-finite values.
Results may differ from a plain program's by a relative error of at most 0.0065.
Values may be sent and summed in bfloat16 or wider, within the bound.
A program may use at most 64 MiB of HBM per device.

v0:
```python
import jax
import jax.numpy as jnp
from jax import lax
from jax.sharding import PartitionSpec as P


def expert_pass(rows_x, rows_o, gate_mat, up_mat, down_mat):
    pre_gate = jnp.dot(rows_x, gate_mat, preferred_element_type=jnp.float32)
    pre_up = jnp.dot(rows_x, up_mat, preferred_element_type=jnp.float32)
    sigma = jax.nn.sigmoid(pre_gate)
    active = pre_gate * sigma
    hidden = (active * pre_up).astype(jnp.bfloat16)
    expert_out = jnp.dot(hidden, down_mat.T, preferred_element_type=jnp.float32).astype(
        jnp.bfloat16
    )
    grad_hidden = jnp.dot(rows_o, down_mat, preferred_element_type=jnp.float32)
    slope = sigma * (1.0 + pre_gate * (1.0 - sigma))
    grad_gate_pre = (grad_hidden * pre_up * slope).astype(jnp.bfloat16)
    grad_up_pre = (grad_hidden * active).astype(jnp.bfloat16)
    grad_rows = (
        jnp.dot(grad_gate_pre, gate_mat.T, preferred_element_type=jnp.float32)
        + jnp.dot(grad_up_pre, up_mat.T, preferred_element_type=jnp.float32)
    ).astype(jnp.bfloat16)
    return (hidden, expert_out, grad_gate_pre, grad_up_pre, grad_rows)


def contract_rows(left, right):
    return lax.dot_general(
        left, right, (((0,), (0,)), ((), ())), preferred_element_type=jnp.float32
    )


def per_device(tokens, cotangent, gate_probs, expert_ids, gate_weight, up_weight, down_weight):
    tok_rows, model_width = tokens.shape
    top_count = expert_ids.shape[1]
    outer_count = lax.axis_size("expouter")
    inner_count = lax.axis_size("expinner")
    expert_count = outer_count * inner_count
    capacity = max(2, tok_rows * top_count * 5 // (4 * expert_count))
    slots_all = expert_count * capacity
    assigns = tok_rows * top_count
    flat_route = expert_ids.reshape(assigns)
    onehot = (flat_route[:, None] == jnp.arange(expert_count, dtype=jnp.int32)[None, :]).astype(
        jnp.int32
    )
    earlier = jnp.cumsum(onehot, axis=0) - onehot
    slot_pos = jnp.sum(earlier * onehot, axis=1)
    target = flat_route * capacity + slot_pos
    select = (target[None, :] == jnp.arange(slots_all, dtype=jnp.int32)[:, None]).astype(
        jnp.bfloat16
    )
    token_select = select.reshape(slots_all, tok_rows, top_count).sum(axis=2)
    send_x = jnp.dot(token_select, tokens, preferred_element_type=jnp.float32).astype(jnp.bfloat16)
    scaled = (gate_probs[:, :, None] * cotangent[:, None, :].astype(jnp.float32)).astype(
        jnp.bfloat16
    )
    send_o = jnp.dot(
        select, scaled.reshape(assigns, model_width), preferred_element_type=jnp.float32
    ).astype(jnp.bfloat16)
    weights_all = (
        lax.all_gather(gate_weight, "dp", axis=1, tiled=True),
        lax.all_gather(up_weight, "dp", axis=1, tiled=True),
        lax.all_gather(down_weight, "dp", axis=1, tiled=True),
    )
    gate_full = weights_all[0][0]
    up_full = weights_all[1][0]
    down_full = weights_all[2][0]
    shaped = (
        send_x.reshape(expert_count, capacity, model_width),
        send_o.reshape(expert_count, capacity, model_width),
    )
    recv_x, recv_o = (
        lax.all_to_all(
            shaped[0], ("expouter", "expinner"), split_axis=0, concat_axis=0, tiled=True
        ),
        lax.all_to_all(
            shaped[1], ("expouter", "expinner"), split_axis=0, concat_axis=0, tiled=True
        ),
    )
    rows_x = recv_x.reshape(slots_all, model_width)
    rows_o = recv_o.reshape(slots_all, model_width)
    hidden, expert_out, grad_gate_pre, grad_up_pre, grad_rows = expert_pass(
        rows_x, rows_o, gate_full, up_full, down_full
    )
    returned = (
        expert_out.reshape(expert_count, capacity, model_width),
        grad_rows.reshape(expert_count, capacity, model_width),
    )
    back_out, back_grad = (
        lax.all_to_all(
            returned[0], ("expouter", "expinner"), split_axis=0, concat_axis=0, tiled=True
        ),
        lax.all_to_all(
            returned[1], ("expouter", "expinner"), split_axis=0, concat_axis=0, tiled=True
        ),
    )
    pick_out = back_out.reshape(slots_all, model_width)[target].reshape(
        tok_rows, top_count, model_width
    )
    pick_grad = back_grad.reshape(slots_all, model_width)[target].reshape(
        tok_rows, top_count, model_width
    )
    pick_float = pick_out.astype(jnp.float32)
    mixed = jnp.sum(gate_probs[:, :, None] * pick_float, axis=1).astype(jnp.bfloat16)
    grad_tokens = jnp.sum(pick_grad.astype(jnp.float32), axis=1).astype(jnp.bfloat16)
    grad_probs = jnp.sum(cotangent[:, None, :].astype(jnp.float32) * pick_float, axis=2)
    cols_x, cols_o = (
        lax.all_to_all(rows_x, "dp", split_axis=1, concat_axis=0, tiled=True),
        lax.all_to_all(rows_o, "dp", split_axis=1, concat_axis=0, tiled=True),
    )
    grad_g = contract_rows(cols_x, lax.all_gather(grad_gate_pre, "dp", axis=0, tiled=True))
    grad_u = contract_rows(cols_x, lax.all_gather(grad_up_pre, "dp", axis=0, tiled=True))
    grad_d = contract_rows(cols_o, lax.all_gather(hidden, "dp", axis=0, tiled=True))
    return (mixed, grad_tokens, grad_probs, grad_g[None], grad_u[None], grad_d[None])


def solution(mesh):
    return jax.shard_map(
        per_device,
        mesh=mesh,
        in_specs=(
            P(("dp", "expouter", "expinner"), None),
            P(("dp", "expouter", "expinner"), None),
            P(("dp", "expouter", "expinner"), None),
            P(("dp", "expouter", "expinner"), None),
            P(("expouter", "expinner"), "dp", None),
            P(("expouter", "expinner"), "dp", None),
            P(("expouter", "expinner"), "dp", None),
        ),
        out_specs=(
            P(("dp", "expouter", "expinner"), None),
            P(("dp", "expouter", "expinner"), None),
            P(("dp", "expouter", "expinner"), None),
            P(("expouter", "expinner"), "dp", None),
            P(("expouter", "expinner"), "dp", None),
            P(("expouter", "expinner"), "dp", None),
        ),
        check_vma=False,
    )
```

profile of v0, /device:TPU:1, one launch (start us, length us, event | category | flops | bytes accessed | tf_op | source)
XLA Modules:
  0.0 330.3 jit_solution(10053245813468858572)
XLA Ops:
  7.2 0.7 all-gather.9.cloned.1.call-update
  7.9 0.8 copy.33
  8.7 0.1 eq.45
  8.8 0.1 eq.49
  9.0 0.6 reduce-window.6
  9.6 0.2 slice_reduce_fusion
  9.8 0.1 fusion.28
  10.0 0.1 reduce_sum.56
  10.1 0.1 copy.37
  10.2 0.1 fusion.24
  10.3 0.3 convolution_convert_fusion
  10.6 1.2 reshape.131
  11.8 19.4 %all-to-all-start = ((bf16[64,5,1024]{2,1,0:T(8,128)(2,1)}), bf16[64,5,1024]{2,1,0:T(8,128)(2,1)S(1)}, u32[]{:S(2)}, u32[]{:S(2)}) async-start(bf16[64,5,1024]{2,1,0:T(8,128)(2,1)} %reshape.131), calls=%async_computation | async-start | bytes 2097152 | tf_op jit(solution)/shard_map/all_to_all | solution.py:73
  31.3 0.0 all-gather.11.cloned.1.call-start
  31.3 0.7 all-gather.11.cloned.1.call-update
  32.0 0.1 copy.32
  32.1 0.1 mul.95
  32.3 0.3 mul.97
  32.6 0.7 mul.98
  33.3 0.4 convolution_convert_fusion.1
  33.7 1.2 reshape.135
  35.0 48.6 %all-to-all-done = bf16[64,5,1024]{2,1,0:T(8,128)(2,1)S(1)} async-done(((bf16[64,5,1024]{2,1,0:T(8,128)(2,1)}), bf16[64,5,1024]{2,1,0:T(8,128)(2,1)S(1)}, u32[]{:S(2)}, u32[]{:S(2)}) %all-to-all-start) | async-done | bytes 655392 | tf_op jit(solution)/shard_map/all_to_all | solution.py:73
  83.6 8.3 %all-to-all-start.2 = ((bf16[64,5,1024]{2,1,0:T(8,128)(2,1)}), bf16[64,5,1024]{2,1,0:T(8,128)(2,1)S(1)}, u32[]{:S(2)}, u32[]{:S(2)}) async-start(bf16[64,5,1024]{2,1,0:T(8,128)(2,1)} %reshape.135), calls=%async_computation.2 | async-start | bytes 2097152 | tf_op jit(solution)/shard_map/all_to_all | solution.py:76
  91.9 0.0 all-gather.7.cloned.1.call-start
  91.9 0.7 all-gather.7.cloned.1.call-update
  92.7 0.3 reshape.132
  92.9 51.8 %all-to-all-done.2 = bf16[64,5,1024]{2,1,0:T(8,128)(2,1)S(1)} async-done(((bf16[64,5,1024]{2,1,0:T(8,128)(2,1)}), bf16[64,5,1024]{2,1,0:T(8,128)(2,1)S(1)}, u32[]{:S(2)}, u32[]{:S(2)}) %all-to-all-start.2) | async-done | bytes 655392 | tf_op jit(solution)/shard_map/all_to_all | solution.py:76
  144.7 1.1 reshape.136
  145.8 3.1 fusion.6
  148.9 3.2 fusion
  152.2 4.1 %multiply_convert_fusion.2 = (bf16[320,768]{1,0:T(8,128)(2,1)}, bf16[320,768]{1,0:T(8,128)(2,1)}, bf16[320,768]{1,0:T(8,128)(2,1)}) fusion(f32[320,768]{1,0:T(8,128)} %fusion, f32[320,768]{1,0:T(8,128)} %fusion.6, bf16[320,1024]{1,0:T(8,128)(2,1)S(1)} %reshape.132, bf16[1,1024,768]{2,1,0:T(8,128)(2,1)} %all-gather.7.cloned.1.call-done), kind=kOutput, calls=%fused_computation.26 | convolution fusion | flops 507002880 | bytes 5668864 | tf_op jit(solution)/shard_map/dot_general | solution.py:8
  156.3 0.0 all-gather.15.cloned.1.call-start
  156.3 0.5 all-gather.15.cloned.1.call-update
  156.9 0.5 all-gather.17.cloned.1.call-update
  157.5 2.3 fusion.4
  159.7 0.7 fusion.18
  160.5 1.2 reshape.137
  161.7 7.4 %all-to-all-start.3 = ((bf16[64,5,1024]{2,1,0:T(8,128)(2,1)}), bf16[64,5,1024]{2,1,0:T(8,128)(2,1)S(1)}, u32[]{:S(2)}, u32[]{:S(2)}) async-start(bf16[64,5,1024]{2,1,0:T(8,128)(2,1)} %reshape.137), calls=%async_computation.3 | async-start | bytes 2097152 | tf_op jit(solution)/shard_map/all_to_all | solution.py:93
  169.0 3.2 fusion.15
  172.2 2.2 reshape.133
  174.4 47.6 %all-to-all-done.3 = bf16[64,5,1024]{2,1,0:T(8,128)(2,1)S(1)} async-done(((bf16[64,5,1024]{2,1,0:T(8,128)(2,1)}), bf16[64,5,1024]{2,1,0:T(8,128)(2,1)S(1)}, u32[]{:S(2)}, u32[]{:S(2)}) %all-to-all-start.3) | async-done | bytes 655392 | tf_op jit(solution)/shard_map/all_to_all | solution.py:93
  222.0 7.4 %all-to-all-start.1 = ((bf16[64,5,1024]{2,1,0:T(8,128)(2,1)}), bf16[64,5,1024]{2,1,0:T(8,128)(2,1)}, u32[]{:S(2)}, u32[]{:S(2)}) async-start(bf16[64,5,1024]{2,1,0:T(8,128)(2,1)} %reshape.133), calls=%async_computation.1 | async-start | bytes 2097152 | tf_op jit(solution)/shard_map/all_to_all | solution.py:90
  229.4 1.8 convert_element_type.67
  231.2 0.1 mul.91
  231.4 1.6 all_to_all.44
  233.0 2.0 copy.39
  235.0 46.0 %all-to-all-done.1 = bf16[64,5,1024]{2,1,0:T(8,128)(2,1)} async-done(((bf16[64,5,1024]{2,1,0:T(8,128)(2,1)}), bf16[64,5,1024]{2,1,0:T(8,128)(2,1)}, u32[]{:S(2)}, u32[]{:S(2)}) %all-to-all-start.1) | async-done | bytes 655392 | tf_op jit(solution)/shard_map/all_to_all | solution.py:90
  280.9 8.3 %all-to-all-start.4 = ((bf16[320,8,128]{2,0,1:T(8,128)(2,1)}), bf16[320,8,128]{2,0,1:T(8,128)(2,1)S(1)}, u32[]{:S(2)}, u32[]{:S(2)}) async-start(bf16[320,8,128]{2,0,1:T(8,128)(2,1)} %copy.39), calls=%async_computation.4 | async-start | bytes 1310720 | tf_op jit(solution)/shard_map/all_to_all | solution.py:108
  289.2 1.6 all_to_all.48
  290.8 2.1 copy.40
  292.9 0.3 reshape.138
  293.2 1.2 gather_fusion.1
  294.3 0.2 reshape.139
  294.5 1.4 reshape.134
  296.0 1.2 gather_fusion
  297.1 0.7 reshape.140
  297.8 3.6 %multiply_reduce_fusion = (f32[128,2]{1,0:T(8,128)S(1)}, bf16[128,1024]{1,0:T(8,128)(2,1)}) fusion(f32[128,2,1024]{2,1,0:T(2,128)S(1)} %reshape.140, f32[128,1024]{1,0:T(8,128)} %convert_element_type.67, f32[128,2]{1,0:T(8,128)S(1)} %copy.32), kind=kLoop, calls=%fused_computation.22 | loop fusion | flops 917248 | bytes 1837056 | tf_op jit(solution)/shard_map/reduce_sum | solution.py:106
  301.4 0.6 copy.41
  302.0 2.1 reduce_sum.60
  304.1 4.8 %all-to-all-start.5 = ((bf16[320,8,128]{2,0,1:T(8,128)(2,1)}), bf16[320,8,128]{2,0,1:T(8,128)(2,1)S(1)}, u32[]{:S(2)}, u32[]{:S(2)}) async-start(bf16[320,8,128]{2,0,1:T(8,128)(2,1)} %copy.40), calls=%async_computation.5 | async-start | bytes 1310720 | tf_op jit(solution)/shard_map/all_to_all | solution.py:109
  308.9 3.6 %convolution_bitcast_fusion.2 = f32[1,128,768]{2,1,0:T(8,128)} fusion(bf16[2560,128]{1,0:T(8,128)(2,1)S(1)} %bitcast.70, bf16[2560,768]{1,0:T(8,128)(2,1)} %all-gather.13.cloned.1.call-done), kind=kOutput, calls=%fused_computation.21 | convolution fusion | flops 503316480 | bytes 4980736 | tf_op jit(solution)/shard_map/dot_general | solution.py:28
  312.5 3.6 %convolution_bitcast_fusion.1 = f32[1,128,768]{2,1,0:T(8,128)} fusion(bf16[2560,128]{1,0:T(8,128)(2,1)S(1)} %bitcast.71, bf16[2560,768]{1,0:T(8,128)(2,1)} %all-gather.15.cloned.1.call-done), kind=kOutput, calls=%fused_computation.20 | convolution fusion | flops 503316480 | bytes 4980736 | tf_op jit(solution)/shard_map/dot_general | solution.py:28
  316.1 3.7 %all-to-all-done.5 = bf16[320,8,128]{2,0,1:T(8,128)(2,1)S(1)} async-done(((bf16[320,8,128]{2,0,1:T(8,128)(2,1)}), bf16[320,8,128]{2,0,1:T(8,128)(2,1)S(1)}, u32[]{:S(2)}, u32[]{:S(2)}) %all-to-all-start.5) | async-done | bytes 655392 | tf_op jit(solution)/shard_map/all_to_all | solution.py:109
  319.8 3.6 %convolution_bitcast_fusion = f32[1,128,768]{2,1,0:T(8,128)} fusion(bf16[2560,128]{1,0:T(8,128)(2,1)S(1)} %bitcast.72, bf16[2560,768]{1,0:T(8,128)(2,1)} %all-gather.17.cloned.1.call-done), kind=kOutput, calls=%fused_computation.19 | convolution fusion | flops 503316480 | bytes 4980736 | tf_op jit(solution)/shard_map/dot_general | solution.py:28
  (30 shorter events, 0.3 us)
Async XLA Ops:
  7.2 3.1 copy-start
  7.2 138.7 %all-gather.9.cloned.1.call-start = ((), (), s32[]{:S(2)}) async-start(), calls=%async_computation.7 | async-start | bytes 1769472 | tf_op jit(solution)/shard_map/all_gather | solution.py:62
  11.8 20.2 %copy-start.5 = (f32[128,2]{0,1:T(2,128)S(1)}, f32[128,2]{0,1:T(2,128)}, u32[]{:S(2)}) copy-start(f32[128,2]{0,1:T(2,128)} %param.9) | copy-start | bytes 3076
  11.8 20.4 %copy-start.4 = (bf16[128,1024]{1,0:T(8,128)(2,1)S(1)}, bf16[128,1024]{1,0:T(8,128)(2,1)}, u32[]{:S(2)}) copy-start(bf16[128,1024]{1,0:T(8,128)(2,1)} %param.8) | copy-start | bytes 786436
  11.8 71.7 %all-to-all-start = ((bf16[64,5,1024]{2,1,0:T(8,128)(2,1)}), bf16[64,5,1024]{2,1,0:T(8,128)(2,1)S(1)}, u32[]{:S(2)}, u32[]{:S(2)}) async-start(bf16[64,5,1024]{2,1,0:T(8,128)(2,1)} %reshape.131), calls=%async_computation | async-start | bytes 2097152 | tf_op jit(solution)/shard_map/all_to_all | solution.py:73
  31.3 117.7 %all-gather.11.cloned.1.call-start = ((), (), s32[]{:S(2)}) async-start(), calls=%async_computation.8 | async-start | bytes 1769472 | tf_op jit(solution)/shard_map/all_gather | solution.py:63
  83.6 61.1 %all-to-all-start.2 = ((bf16[64,5,1024]{2,1,0:T(8,128)(2,1)}), bf16[64,5,1024]{2,1,0:T(8,128)(2,1)S(1)}, u32[]{:S(2)}, u32[]{:S(2)}) async-start(bf16[64,5,1024]{2,1,0:T(8,128)(2,1)} %reshape.135), calls=%async_computation.2 | async-start | bytes 2097152 | tf_op jit(solution)/shard_map/all_to_all | solution.py:76
  91.9 60.3 %all-gather.7.cloned.1.call-start = ((), (), s32[]{:S(2)}) async-start(), calls=%async_computation.6 | async-start | bytes 1769472 | tf_op jit(solution)/shard_map/all_gather | solution.py:61
  92.6 216.3 %all-gather.13.cloned.1.call-start = ((), (), s32[]{:S(2)}) async-start(), calls=%async_computation.9 | async-start | bytes 4423680 | tf_op jit(solution)/shard_map/all_gather | solution.py:111
  156.2 1.2 copy-start.1
  156.3 156.3 %all-gather.15.cloned.1.call-start = ((), (), s32[]{:S(2)}) async-start(), calls=%async_computation.10 | async-start | bytes 4423680 | tf_op jit(solution)/shard_map/all_gather | solution.py:112
  156.9 163.0 %all-gather.17.cloned.1.call-start = ((), (), s32[]{:S(2)}) async-start(), calls=%async_computation.11 | async-start | bytes 4423680 | tf_op jit(solution)/shard_map/all_gather | solution.py:113
  157.4 2.3 copy-start.2
  157.4 2.3 copy-start.3
  161.7 60.3 %all-to-all-start.3 = ((bf16[64,5,1024]{2,1,0:T(8,128)(2,1)}), bf16[64,5,1024]{2,1,0:T(8,128)(2,1)S(1)}, u32[]{:S(2)}, u32[]{:S(2)}) async-start(bf16[64,5,1024]{2,1,0:T(8,128)(2,1)} %reshape.137), calls=%async_computation.3 | async-start | bytes 2097152 | tf_op jit(solution)/shard_map/all_to_all | solution.py:93
  222.0 59.0 %all-to-all-start.1 = ((bf16[64,5,1024]{2,1,0:T(8,128)(2,1)}), bf16[64,5,1024]{2,1,0:T(8,128)(2,1)}, u32[]{:S(2)}, u32[]{:S(2)}) async-start(bf16[64,5,1024]{2,1,0:T(8,128)(2,1)} %reshape.133), calls=%async_computation.1 | async-start | bytes 2097152 | tf_op jit(solution)/shard_map/all_to_all | solution.py:90
  280.9 23.2 %all-to-all-start.4 = ((bf16[320,8,128]{2,0,1:T(8,128)(2,1)}), bf16[320,8,128]{2,0,1:T(8,128)(2,1)S(1)}, u32[]{:S(2)}, u32[]{:S(2)}) async-start(bf16[320,8,128]{2,0,1:T(8,128)(2,1)} %copy.39), calls=%async_computation.4 | async-start | bytes 1310720 | tf_op jit(solution)/shard_map/all_to_all | solution.py:108
  304.1 15.7 %all-to-all-start.5 = ((bf16[320,8,128]{2,0,1:T(8,128)(2,1)}), bf16[320,8,128]{2,0,1:T(8,128)(2,1)S(1)}, u32[]{:S(2)}, u32[]{:S(2)}) async-start(bf16[320,8,128]{2,0,1:T(8,128)(2,1)} %copy.40), calls=%async_computation.5 | async-start | bytes 1310720 | tf_op jit(solution)/shard_map/all_to_all | solution.py:109
Sparse Core Ops, SparseCore 0:
  10.1 37.8 all-gather.8
  50.2 32.1 all-gather.10
  94.8 34.0 all-gather.6
  156.4 33.3 all-gather.12
  191.8 38.6 all-gather.14
  232.5 38.6 all-gather.16
where the time goes:
time: 331 us; the launch traced here: 330 us
  waiting for transfers between devices  201 us (61%)
  starting transfers between devices  55.8 us (17%)
  matrix products  28 us (8%)
  local copies, waits for them, and re-layouts  22.9 us (7%)
  between operations  14.4 us (4%)
  other arithmetic  8.38 us (3%)
    all_to_all x1, waiting for transfers between devices, per_device(): lax.all_to_all(shaped[1], ('expouter', 'expinner'), split_axis=0, concat_...  51.8 us
    all_to_all x1, waiting for transfers between devices, per_device(): lax.all_to_all(shaped[0], ('expouter', 'expinner'), split_axis=0, concat_...  48.6 us
    all_to_all x1, waiting for transfers between devices, per_device(): lax.all_to_all(returned[1], ('expouter', 'expinner'), split_axis=0, conca...  47.6 us
    all_to_all x1, waiting for transfers between devices, per_device(): lax.all_to_all(returned[0], ('expouter', 'expinner'), split_axis=0, conca...  46 us
    all_to_all x1, starting transfers between devices, per_device(): lax.all_to_all(shaped[0], ('expouter', 'expinner'), split_axis=0, concat_...  19.4 us
    dot_general x3, matrix products, contract_rows(): lax.dot_general(left, right, (((0,), (0,)), ((), ())), preferred_element_...  10.8 us
    all_to_all x1, starting transfers between devices, per_device(): lax.all_to_all(shaped[1], ('expouter', 'expinner'), split_axis=0, concat_...  8.28 us
    all_to_all x1, starting transfers between devices, per_device(): lax.all_to_all(rows_x, 'dp', split_axis=1, concat_axis=0, tiled=True)  8.27 us
  transfers between devices with their start and end apart: 12, of which 5 were waited for; matrix products, arithmetic and copies ran while one was open for 15% of the time, Pallas kernels for 0%

commit v1 on v0

--- a/solution.py
+++ b/solution.py
@@ -40,11 +40,9 @@
     slots_all = expert_count * capacity
     assigns = tok_rows * top_count
     flat_route = expert_ids.reshape(assigns)
-    onehot = (flat_route[:, None] == jnp.arange(expert_count, dtype=jnp.int32)[None, :]).astype(
-        jnp.int32
-    )
-    earlier = jnp.cumsum(onehot, axis=0) - onehot
-    slot_pos = jnp.sum(earlier * onehot, axis=1)
+    order = jnp.arange(assigns, dtype=jnp.int32)
+    before = (order[None, :] < order[:, None]) & (flat_route[None, :] == flat_route[:, None])
+    slot_pos = jnp.sum(before.astype(jnp.int32), axis=1)
     target = flat_route * capacity + slot_pos
     select = (target[None, :] == jnp.arange(slots_all, dtype=jnp.int32)[:, None]).astype(
         jnp.bfloat16

time: 331 us -> 330 us (level)
  transfers between devices with their start and end apart: 12 -> 12, of which waited for: 5 -> 5; matrix products, arithmetic and copies ran while one was open for 15% -> 14% of each run, Pallas kernels for 0% -> 0%
where the time goes in v1:
time: 330 us; the launch traced here: 329 us
  waiting for transfers between devices  201 us (61%)
  starting transfers between devices  55.7 us (17%)
  matrix products  28 us (8%)
  local copies, waits for them, and re-layouts  22.6 us (7%)
  between operations  14.4 us (4%)
  other arithmetic  7.8 us (2%)
    all_to_all x1, waiting for transfers between devices, per_device(): lax.all_to_all(shaped[1], ('expouter', 'expinner'), split_axis=0, concat_...  51.8 us
    all_to_all x1, waiting for transfers between devices, per_device(): lax.all_to_all(shaped[0], ('expouter', 'expinner'), split_axis=0, concat_...  48.6 us
    all_to_all x1, waiting for transfers between devices, per_device(): lax.all_to_all(returned[1], ('expouter', 'expinner'), split_axis=0, conca...  47.7 us
    all_to_all x1, waiting for transfers between devices, per_device(): lax.all_to_all(returned[0], ('expouter', 'expinner'), split_axis=0, conca...  46 us
    all_to_all x1, starting transfers between devices, per_device(): lax.all_to_all(shaped[0], ('expouter', 'expinner'), split_axis=0, concat_...  19.4 us
    dot_general x3, matrix products, contract_rows(): lax.dot_general(left, right, (((0,), (0,)), ((), ())), preferred_element_...  10.8 us
    all_to_all x1, starting transfers between devices, per_device(): lax.all_to_all(shaped[1], ('expouter', 'expinner'), split_axis=0, concat_...  8.38 us
    all_to_all x1, starting transfers between devices, per_device(): lax.all_to_all(rows_x, 'dp', split_axis=1, concat_axis=0, tiled=True)  8.13 us
  transfers between devices with their start and end apart: 12, of which 5 were waited for; matrix products, arithmetic and copies ran while one was open for 14% of the time, Pallas kernels for 0%

profile of v1, /device:TPU:1, one launch (start us, length us, event | category | flops | bytes accessed | tf_op | source)
XLA Modules:
  0.0 329.3 jit_solution(1604184112315230597)
XLA Ops:
  7.2 0.0 all-gather.9.cloned.1.call-start
  7.2 0.7 all-gather.9.cloned.1.call-update
  7.9 0.8 copy.29
  8.7 0.1 eq.35
  8.8 0.2 convert_reduce_fusion
  9.0 0.1 reduce_sum.56
  9.2 0.1 copy.31
  9.3 0.1 fusion.25
  9.3 0.3 convolution_convert_fusion
  9.7 1.2 reshape.115
  10.9 19.4 %all-to-all-start = ((bf16[64,5,1024]{2,1,0:T(8,128)(2,1)}), bf16[64,5,1024]{2,1,0:T(8,128)(2,1)S(1)}, u32[]{:S(2)}, u32[]{:S(2)}) async-start(bf16[64,5,1024]{2,1,0:T(8,128)(2,1)} %reshape.115), calls=%async_computation | async-start | bytes 2097152 | tf_op jit(solution)/shard_map/all_to_all | solution.py:71
  30.3 0.0 all-gather.11.cloned.1.call-start
  30.4 0.7 all-gather.11.cloned.1.call-update
  31.1 0.1 copy.28
  31.2 0.1 mul.91
  31.3 0.3 mul.93
  31.6 0.7 mul.94
  32.4 0.4 convolution_convert_fusion.1
  32.8 1.2 reshape.119
  34.0 48.6 %all-to-all-done = bf16[64,5,1024]{2,1,0:T(8,128)(2,1)S(1)} async-done(((bf16[64,5,1024]{2,1,0:T(8,128)(2,1)}), bf16[64,5,1024]{2,1,0:T(8,128)(2,1)S(1)}, u32[]{:S(2)}, u32[]{:S(2)}) %all-to-all-start) | async-done | bytes 655392 | tf_op jit(solution)/shard_map/all_to_all | solution.py:71
  82.6 8.4 %all-to-all-start.2 = ((bf16[64,5,1024]{2,1,0:T(8,128)(2,1)}), bf16[64,5,1024]{2,1,0:T(8,128)(2,1)S(1)}, u32[]{:S(2)}, u32[]{:S(2)}) async-start(bf16[64,5,1024]{2,1,0:T(8,128)(2,1)} %reshape.119), calls=%async_computation.2 | async-start | bytes 2097152 | tf_op jit(solution)/shard_map/all_to_all | solution.py:74
  91.0 0.0 all-gather.7.cloned.1.call-start
  91.1 0.7 all-gather.7.cloned.1.call-update
  91.8 0.0 all-gather.13.cloned.1.call-start
  91.8 0.3 reshape.116
  92.1 51.8 %all-to-all-done.2 = bf16[64,5,1024]{2,1,0:T(8,128)(2,1)S(1)} async-done(((bf16[64,5,1024]{2,1,0:T(8,128)(2,1)}), bf16[64,5,1024]{2,1,0:T(8,128)(2,1)S(1)}, u32[]{:S(2)}, u32[]{:S(2)}) %all-to-all-start.2) | async-done | bytes 655392 | tf_op jit(solution)/shard_map/all_to_all | solution.py:74
  143.9 1.1 reshape.120
  145.0 3.0 fusion.6
  148.0 3.3 fusion
  151.3 4.1 %multiply_convert_fusion.2 = (bf16[320,768]{1,0:T(8,128)(2,1)}, bf16[320,768]{1,0:T(8,128)(2,1)}, bf16[320,768]{1,0:T(8,128)(2,1)}) fusion(f32[320,768]{1,0:T(8,128)} %fusion, f32[320,768]{1,0:T(8,128)} %fusion.6, bf16[320,1024]{1,0:T(8,128)(2,1)S(1)} %reshape.116, bf16[1,1024,768]{2,1,0:T(8,128)(2,1)} %all-gather.7.cloned.1.call-done), kind=kOutput, calls=%fused_computation.26 | convolution fusion | flops 507002880 | bytes 5668864 | tf_op jit(solution)/shard_map/dot_general | solution.py:8
  155.4 0.0 all-gather.15.cloned.1.call-start
  155.4 0.5 all-gather.15.cloned.1.call-update
  156.0 0.0 all-gather.17.cloned.1.call-start
  156.0 0.5 all-gather.17.cloned.1.call-update
  156.6 2.2 fusion.4
  158.9 0.7 fusion.18
  159.6 1.3 reshape.121
  160.8 7.4 %all-to-all-start.3 = ((bf16[64,5,1024]{2,1,0:T(8,128)(2,1)}), bf16[64,5,1024]{2,1,0:T(8,128)(2,1)S(1)}, u32[]{:S(2)}, u32[]{:S(2)}) async-start(bf16[64,5,1024]{2,1,0:T(8,128)(2,1)} %reshape.121), calls=%async_computation.3 | async-start | bytes 2097152 | tf_op jit(solution)/shard_map/all_to_all | solution.py:91
  168.2 3.1 fusion.15
  171.4 2.1 reshape.117
  173.5 47.7 %all-to-all-done.3 = bf16[64,5,1024]{2,1,0:T(8,128)(2,1)S(1)} async-done(((bf16[64,5,1024]{2,1,0:T(8,128)(2,1)}), bf16[64,5,1024]{2,1,0:T(8,128)(2,1)S(1)}, u32[]{:S(2)}, u32[]{:S(2)}) %all-to-all-start.3) | async-done | bytes 655392 | tf_op jit(solution)/shard_map/all_to_all | solution.py:91
  221.2 7.4 %all-to-all-start.1 = ((bf16[64,5,1024]{2,1,0:T(8,128)(2,1)}), bf16[64,5,1024]{2,1,0:T(8,128)(2,1)}, u32[]{:S(2)}, u32[]{:S(2)}) async-start(bf16[64,5,1024]{2,1,0:T(8,128)(2,1)} %reshape.117), calls=%async_computation.1 | async-start | bytes 2097152 | tf_op jit(solution)/shard_map/all_to_all | solution.py:88
  228.6 1.8 convert_element_type.62
  230.4 0.1 mul.87
  230.5 1.6 all_to_all.44
  232.1 2.0 copy.33
  234.2 46.0 %all-to-all-done.1 = bf16[64,5,1024]{2,1,0:T(8,128)(2,1)} async-done(((bf16[64,5,1024]{2,1,0:T(8,128)(2,1)}), bf16[64,5,1024]{2,1,0:T(8,128)(2,1)}, u32[]{:S(2)}, u32[]{:S(2)}) %all-to-all-start.1) | async-done | bytes 655392 | tf_op jit(solution)/shard_map/all_to_all | solution.py:88
  280.1 8.1 %all-to-all-start.4 = ((bf16[320,8,128]{2,0,1:T(8,128)(2,1)}), bf16[320,8,128]{2,0,1:T(8,128)(2,1)S(1)}, u32[]{:S(2)}, u32[]{:S(2)}) async-start(bf16[320,8,128]{2,0,1:T(8,128)(2,1)} %copy.33), calls=%async_computation.4 | async-start | bytes 1310720 | tf_op jit(solution)/shard_map/all_to_all | solution.py:106
  288.3 1.6 all_to_all.48
  289.9 2.0 copy.34
  291.9 0.3 reshape.122
  292.2 1.2 gather_fusion.1
  293.4 0.2 reshape.123
  293.6 1.4 reshape.118
  295.0 1.2 gather_fusion
  296.2 0.7 reshape.124
  296.8 3.6 %multiply_reduce_fusion = (f32[128,2]{1,0:T(8,128)S(1)}, bf16[128,1024]{1,0:T(8,128)(2,1)}) fusion(f32[128,2,1024]{2,1,0:T(2,128)S(1)} %reshape.124, f32[128,1024]{1,0:T(8,128)} %convert_element_type.62, f32[128,2]{1,0:T(8,128)S(1)} %copy.28), kind=kLoop, calls=%fused_computation.22 | loop fusion | flops 917248 | bytes 1837056 | tf_op jit(solution)/shard_map/reduce_sum | solution.py:104
  300.4 0.6 copy.35
  301.1 2.1 reduce_sum.60
  303.2 4.8 %all-to-all-start.5 = ((bf16[320,8,128]{2,0,1:T(8,128)(2,1)}), bf16[320,8,128]{2,0,1:T(8,128)(2,1)S(1)}, u32[]{:S(2)}, u32[]{:S(2)}) async-start(bf16[320,8,128]{2,0,1:T(8,128)(2,1)} %copy.34), calls=%async_computation.5 | async-start | bytes 1310720 | tf_op jit(solution)/shard_map/all_to_all | solution.py:107
  308.0 3.6 %convolution_bitcast_fusion.2 = f32[1,128,768]{2,1,0:T(8,128)} fusion(bf16[2560,128]{1,0:T(8,128)(2,1)S(1)} %bitcast.51, bf16[2560,768]{1,0:T(8,128)(2,1)} %all-gather.13.cloned.1.call-done), kind=kOutput, calls=%fused_computation.21 | convolution fusion | flops 503316480 | bytes 4980736 | tf_op jit(solution)/shard_map/dot_general | solution.py:28
  311.6 3.6 %convolution_bitcast_fusion.1 = f32[1,128,768]{2,1,0:T(8,128)} fusion(bf16[2560,128]{1,0:T(8,128)(2,1)S(1)} %bitcast.52, bf16[2560,768]{1,0:T(8,128)(2,1)} %all-gather.15.cloned.1.call-done), kind=kOutput, calls=%fused_computation.20 | convolution fusion | flops 503316480 | bytes 4980736 | tf_op jit(solution)/shard_map/dot_general | solution.py:28
  315.2 3.7 %all-to-all-done.5 = bf16[320,8,128]{2,0,1:T(8,128)(2,1)S(1)} async-done(((bf16[320,8,128]{2,0,1:T(8,128)(2,1)}), bf16[320,8,128]{2,0,1:T(8,128)(2,1)S(1)}, u32[]{:S(2)}, u32[]{:S(2)}) %all-to-all-start.5) | async-done | bytes 655392 | tf_op jit(solution)/shard_map/all_to_all | solution.py:107
  318.9 3.6 %convolution_bitcast_fusion = f32[1,128,768]{2,1,0:T(8,128)} fusion(bf16[2560,128]{1,0:T(8,128)(2,1)S(1)} %bitcast.53, bf16[2560,768]{1,0:T(8,128)(2,1)} %all-gather.17.cloned.1.call-done), kind=kOutput, calls=%fused_computation.19 | convolution fusion | flops 503316480 | bytes 4980736 | tf_op jit(solution)/shard_map/dot_general | solution.py:28
  (24 shorter events, 0.1 us)
Async XLA Ops:
  7.2 2.2 copy-start
  7.2 137.8 %all-gather.9.cloned.1.call-start = ((), (), s32[]{:S(2)}) async-start(), calls=%async_computation.7 | async-start | bytes 1769472 | tf_op jit(solution)/shard_map/all_gather | solution.py:60
  10.9 20.2 %copy-start.5 = (f32[128,2]{0,1:T(2,128)S(1)}, f32[128,2]{0,1:T(2,128)}, u32[]{:S(2)}) copy-start(f32[128,2]{0,1:T(2,128)} %param.9) | copy-start | bytes 3076
  10.9 20.4 %copy-start.4 = (bf16[128,1024]{1,0:T(8,128)(2,1)S(1)}, bf16[128,1024]{1,0:T(8,128)(2,1)}, u32[]{:S(2)}) copy-start(bf16[128,1024]{1,0:T(8,128)(2,1)} %param.8) | copy-start | bytes 786436
  10.9 71.8 %all-to-all-start = ((bf16[64,5,1024]{2,1,0:T(8,128)(2,1)}), bf16[64,5,1024]{2,1,0:T(8,128)(2,1)S(1)}, u32[]{:S(2)}, u32[]{:S(2)}) async-start(bf16[64,5,1024]{2,1,0:T(8,128)(2,1)} %reshape.115), calls=%async_computation | async-start | bytes 2097152 | tf_op jit(solution)/shard_map/all_to_all | solution.py:71
  30.3 117.7 %all-gather.11.cloned.1.call-start = ((), (), s32[]{:S(2)}) async-start(), calls=%async_computation.8 | async-start | bytes 1769472 | tf_op jit(solution)/shard_map/all_gather | solution.py:61
  82.6 61.2 %all-to-all-start.2 = ((bf16[64,5,1024]{2,1,0:T(8,128)(2,1)}), bf16[64,5,1024]{2,1,0:T(8,128)(2,1)S(1)}, u32[]{:S(2)}, u32[]{:S(2)}) async-start(bf16[64,5,1024]{2,1,0:T(8,128)(2,1)} %reshape.119), calls=%async_computation.2 | async-start | bytes 2097152 | tf_op jit(solution)/shard_map/all_to_all | solution.py:74
  91.0 60.3 %all-gather.7.cloned.1.call-start = ((), (), s32[]{:S(2)}) async-start(), calls=%async_computation.6 | async-start | bytes 1769472 | tf_op jit(solution)/shard_map/all_gather | solution.py:59
  91.8 216.2 %all-gather.13.cloned.1.call-start = ((), (), s32[]{:S(2)}) async-start(), calls=%async_computation.9 | async-start | bytes 4423680 | tf_op jit(solution)/shard_map/all_gather | solution.py:109
  155.4 1.2 copy-start.1
  155.4 156.2 %all-gather.15.cloned.1.call-start = ((), (), s32[]{:S(2)}) async-start(), calls=%async_computation.10 | async-start | bytes 4423680 | tf_op jit(solution)/shard_map/all_gather | solution.py:110
  156.0 162.9 %all-gather.17.cloned.1.call-start = ((), (), s32[]{:S(2)}) async-start(), calls=%async_computation.11 | async-start | bytes 4423680 | tf_op jit(solution)/shard_map/all_gather | solution.py:111
  156.6 2.3 copy-start.2
  156.6 2.3 copy-start.3
  160.8 60.4 %all-to-all-start.3 = ((bf16[64,5,1024]{2,1,0:T(8,128)(2,1)}), bf16[64,5,1024]{2,1,0:T(8,128)(2,1)S(1)}, u32[]{:S(2)}, u32[]{:S(2)}) async-start(bf16[64,5,1024]{2,1,0:T(8,128)(2,1)} %reshape.121), calls=%async_computation.3 | async-start | bytes 2097152 | tf_op jit(solution)/shard_map/all_to_all | solution.py:91
  221.2 58.9 %all-to-all-start.1 = ((bf16[64,5,1024]{2,1,0:T(8,128)(2,1)}), bf16[64,5,1024]{2,1,0:T(8,128)(2,1)}, u32[]{:S(2)}, u32[]{:S(2)}) async-start(bf16[64,5,1024]{2,1,0:T(8,128)(2,1)} %reshape.117), calls=%async_computation.1 | async-start | bytes 2097152 | tf_op jit(solution)/shard_map/all_to_all | solution.py:88
  280.1 23.0 %all-to-all-start.4 = ((bf16[320,8,128]{2,0,1:T(8,128)(2,1)}), bf16[320,8,128]{2,0,1:T(8,128)(2,1)S(1)}, u32[]{:S(2)}, u32[]{:S(2)}) async-start(bf16[320,8,128]{2,0,1:T(8,128)(2,1)} %copy.33), calls=%async_computation.4 | async-start | bytes 1310720 | tf_op jit(solution)/shard_map/all_to_all | solution.py:106
  303.2 15.7 %all-to-all-start.5 = ((bf16[320,8,128]{2,0,1:T(8,128)(2,1)}), bf16[320,8,128]{2,0,1:T(8,128)(2,1)S(1)}, u32[]{:S(2)}, u32[]{:S(2)}) async-start(bf16[320,8,128]{2,0,1:T(8,128)(2,1)} %copy.34), calls=%async_computation.5 | async-start | bytes 1310720 | tf_op jit(solution)/shard_map/all_to_all | solution.py:107
Sparse Core Ops, SparseCore 0:
  10.1 37.8 all-gather.8
  50.2 32.1 all-gather.10
  94.0 33.9 all-gather.6
  155.5 33.2 all-gather.12
  190.8 38.6 all-gather.14
  231.5 38.6 all-gather.16

commit v2 on v1

v2 whole, which is shorter than its diff:
```python
import functools

import jax
import jax.numpy as jnp
from jax import lax
from jax.experimental import pallas as pl
from jax.experimental.pallas import tpu as pltpu
from jax.sharding import PartitionSpec as P

MESH = pl.DeviceIdType.MESH
F32 = jnp.float32
BF16 = jnp.bfloat16
LANES = 128
NY = 4
CAP = 5


def fifth(v):
    return (v * 52429) >> 18


def kernel(
    nx, nz_lo, nz_hi, ny,
    tok, cot, probs, ids, wg, wu, wd,
    mixed, gtok, gprob, og, ou, od,
    weights, send, recv, rsend, rrecv, wide, xo, acts, scaled,
    csend, crecv, xsend, xrecv, acc, back,
    load_sem, fs_sem, fr_sem, rs_sem, rr_sem,
    wxs_sem, wxr_sem, wcs_sem, wcr_sem,
    gcs_sem, gcr_sem, gxs_sem, gxr_sem,
):
    nz = nz_lo * nz_hi
    width = tok.shape[1]
    chunks = width // LANES
    tall = 2 * chunks
    group = nz * CAP
    hidden_n = wg.shape[2]
    me = lax.axis_index("dp")
    x, core = me // 2, me % 2
    inner = lax.axis_index("expinner")
    y = inner % ny
    z = (inner // ny) * nz_lo + lax.axis_index("expouter")

    def at_yz(dy, dz):
        tz = lax.rem(z + dz + nz, nz)
        ty = lax.rem(y + dy + ny, ny)
        return {"expouter": lax.rem(tz, nz_lo), "expinner": (tz // nz_lo) * ny + ty}

    def at_x(dx):
        return {"dp": lax.rem(x + dx, nx) * 2 + core}

    twin = {"dp": x * 2 + 1 - core}

    def remote(src, dst, ss, rs, device):
        return pltpu.make_async_remote_copy(
            src_ref=src, dst_ref=dst, send_sem=ss, recv_sem=rs,
            device_id=device, device_id_type=MESH,
        )

    own = [pltpu.make_async_copy(w.at[0], weights.at[m, me], load_sem.at[m]) for m, w in enumerate((wg, wu, wd))]
    for copy in own:
        copy.start()
    barrier = pltpu.get_barrier_semaphore()

    def greet(i, _):
        pl.semaphore_signal(barrier, inc=1, device_id=at_yz(i // nz, lax.rem(i, nz)), device_id_type=MESH)
        return 0

    lax.fori_loop(1, ny * nz, greet, 0)
    for dx in range(1, nx):
        pl.semaphore_signal(barrier, inc=1, device_id=at_x(dx), device_id_type=MESH)
    pl.semaphore_signal(barrier, inc=1, device_id=twin, device_id_type=MESH)

    rows = tok.shape[0]
    idf = ids[...].astype(F32)
    down_id = [jnp.broadcast_to(idf[:, k:k + 1], (rows, rows)) for k in range(2)]
    over_id = [jnp.transpose(b) for b in down_id]
    first = lax.broadcasted_iota(jnp.int32, (rows, rows), 0)
    second = lax.broadcasted_iota(jnp.int32, (rows, rows), 1)
    col_target, row_target = [], []
    for k in range(2):
        hits = sum(jnp.where((down_id[k] == over_id[j]) & (second < first), 1.0, 0.0) for j in range(2))
        col_target.append(idf[:, k:k + 1] * CAP + jnp.sum(hits, axis=1, keepdims=True))
        hits = sum(jnp.where((down_id[j] == over_id[k]) & (first < second), 1.0, 0.0) for j in range(2))
        row_target.append(over_id[k][0:1, :] * CAP + jnp.sum(hits, axis=0, keepdims=True))
    pr = [probs[:, k:k + 1] for k in range(2)]
    for k in range(2):
        scaled[k * rows:(k + 1) * rows, :] = (pr[k] * cot[...].astype(F32)).astype(BF16)

    def slot_id(dy, q, slot):
        tz = (z + q) & (nz - 1)
        ty = (y + dy) & (ny - 1)
        expert = (tz & (nz_lo - 1)) * (nz_hi * ny) + (tz // nz_lo) * ny + ty
        return (expert * CAP + slot).astype(F32)

    line = lax.broadcasted_iota(jnp.int32, (group, 1), 0)
    line_dz = fifth(line)
    line_slot = line - CAP * line_dz

    def pack(dy):
        wanted = slot_id(dy, line_dz, line_slot)
        sel = [jnp.where(wanted == row_target[k], 1.0, 0.0) for k in range(2)]
        both = (sel[0] + sel[1]).astype(BF16)
        each = jnp.concatenate(sel, axis=1).astype(BF16)
        rows_x = jnp.dot(both, tok[...], preferred_element_type=F32)
        rows_o = jnp.dot(each, scaled[...], preferred_element_type=F32)
        for c in range(chunks):
            cols = slice(c * LANES, (c + 1) * LANES)
            wide[pl.ds(c, group, stride=tall), :] = rows_x[:, cols]
            wide[pl.ds(chunks + c, group, stride=tall), :] = rows_o[:, cols]
        send[pl.ds(dy * nz, nz)] = wide[...].astype(BF16).reshape(nz, CAP * tall, LANES)

    def scatter(dy, src, dst, ss, rs, sign):
        def one(dz, _):
            i = dy * nz + dz

            @pl.when(i > 0)
            def _():
                remote(src.at[i], dst.at[i], ss, rs.at[dy], at_yz(sign * dy, sign * dz)).start()

            return 0

        lax.fori_loop(0, nz, one, 0)

        @pl.when(dy == 0)
        def _():
            pltpu.make_async_copy(src.at[0], dst.at[0], rs.at[0]).start()

    pack(jnp.int32(0))
    for copy in own:
        copy.wait()
    pl.semaphore_wait(barrier, ny * nz - 1 + nx - 1 + 1)

    mine = weights.at[:, me]
    remote(mine, mine, wcs_sem.at[0], wcr_sem.at[0], twin).start()
    for dx in range(1, nx):
        remote(mine, mine, wxs_sem.at[dx], wxr_sem.at[dx], at_x(dx)).start()

    scatter(jnp.int32(0), send, recv, fs_sem, fr_sem, 1)

    def pack_and_send(dy, _):
        pack(dy)
        scatter(dy, send, recv, fs_sem, fr_sem, 1)
        return 0

    lax.fori_loop(1, ny, pack_and_send, 0)

    for dx in range(1, nx):
        theirs = weights.at[:, lax.rem(x - dx + nx, nx) * 2 + core]
        remote(theirs, theirs, wxs_sem.at[dx], wxr_sem.at[dx], at_x(dx)).wait_recv()
        remote(theirs, theirs, wcs_sem.at[dx], wcr_sem.at[dx], twin).start()
    for dx in range(nx):
        theirs = weights.at[:, lax.rem(x - dx + nx, nx) * 2 + 1 - core]
        remote(theirs, theirs, wcs_sem.at[dx], wcr_sem.at[dx], twin).wait_recv()

    def unpack(buf, dy, out):
        wide[...] = buf[pl.ds(dy * nz, nz)].reshape(nz * CAP * tall, LANES).astype(F32)
        here = pl.ds(pl.multiple_of(dy * group, 16), group)
        for part in range(2):
            for c in range(chunks):
                out[part, c, here, :] = wide[pl.ds(part * chunks + c, group, stride=tall), :].astype(BF16)

    step = 256

    def expert(dy, _):
        remote(
            recv.at[pl.ds(dy * nz, nz)], recv.at[pl.ds(dy * nz, nz)], fs_sem, fr_sem.at[dy], twin
        ).wait_recv()
        unpack(recv, dy, xo)
        here = pl.ds(pl.multiple_of(dy * group, 16), group)
        rows_x = jnp.concatenate([xo[0, c, here, :] for c in range(chunks)], axis=1)
        rows_o = jnp.concatenate([xo[1, c, here, :] for c in range(chunks)], axis=1)

        def up(n, _):
            cols = pl.ds(pl.multiple_of(n * step, step), step)
            gate = jnp.dot(rows_x, weights[0, :, :, cols].reshape(width, step), preferred_element_type=F32)
            lift = jnp.dot(rows_x, weights[1, :, :, cols].reshape(width, step), preferred_element_type=F32)
            grad = jnp.dot(rows_o, weights[2, :, :, cols].reshape(width, step), preferred_element_type=F32)
            sigma = jax.nn.sigmoid(gate)
            active = gate * sigma
            slope = sigma * (1.0 + gate * (1.0 - sigma))
            acts[0, here, cols] = (grad * lift * slope).astype(BF16)
            acts[1, here, cols] = (grad * active).astype(BF16)
            acts[2, here, cols] = (active * lift).astype(BF16)
            return 0

        lax.fori_loop(0, hidden_n // step, up, 0)

        def turned(a, m, d):
            w = weights[m, pl.ds(d * 2, 2)].reshape(2 * LANES, hidden_n)
            return lax.dot_general(a, w, (((1,), (1,)), ((), ())), preferred_element_type=F32)

        def down(d, _):
            out = turned(acts[2, here, :], 2, d)
            grad = turned(acts[0, here, :], 0, d) + turned(acts[1, here, :], 1, d)
            for h in range(2):
                cols = slice(h * LANES, (h + 1) * LANES)
                wide[pl.ds(2 * d + h, group, stride=tall), :] = out[:, cols]
                wide[pl.ds(chunks + 2 * d + h, group, stride=tall), :] = grad[:, cols]
            return 0

        lax.fori_loop(0, chunks // 2, down, 0)
        rsend[pl.ds(dy * nz, nz)] = wide[...].astype(BF16).reshape(nz, CAP * tall, LANES)
        scatter(dy, rsend, rrecv, rs_sem, rr_sem, -1)
        return 0

    lax.fori_loop(0, ny, expert, 0)

    def partial(m, shard):
        return lax.dot_general(
            xo[m // 2, shard], acts[m], (((0,), (0,)), ((), ())), preferred_element_type=F32
        )

    def to_twin(i, _):
        dx, m = lax.rem(i // 3 + 1, nx), lax.rem(i, 3)
        csend[i] = partial(m, lax.rem(x + dx, nx) * 2 + 1 - core).astype(BF16)
        remote(csend.at[i], crecv.at[i], gcs_sem.at[i], gcr_sem.at[i], twin).start()
        return 0

    lax.fori_loop(0, 3 * nx, to_twin, 0)

    def along_x(i, _):
        dx, m = lax.rem(i // 3 + 1, nx), lax.rem(i, 3)
        total = partial(m, lax.rem(x + dx, nx) * 2 + core)
        remote(csend.at[i], crecv.at[i], gcs_sem.at[i], gcr_sem.at[i], twin).wait()
        total = total + crecv[i].astype(F32)

        @pl.when(dx > 0)
        def _():
            xsend[i] = total.astype(BF16)
            remote(xsend.at[i], xrecv.at[i], gxs_sem.at[i], gxr_sem.at[i], at_x(dx)).start()

        @pl.when(dx == 0)
        def _():
            acc[m] = total

        return 0

    lax.fori_loop(0, 3 * nx, along_x, 0)

    def returned(dy, _):
        remote(
            rrecv.at[pl.ds(dy * nz, nz)], rrecv.at[pl.ds(dy * nz, nz)], rs_sem, rr_sem.at[dy], twin
        ).wait_recv()
        unpack(rrecv, dy, back)
        return 0

    lax.fori_loop(0, ny - 1, returned, 0)

    def collect(i, _):
        remote(xsend.at[i], xrecv.at[i], gxs_sem.at[i], gxr_sem.at[i], at_x(lax.rem(i // 3 + 1, nx))).wait()
        m = lax.rem(i, 3)
        acc[m] = acc[m] + xrecv[i].astype(F32)
        return 0

    lax.fori_loop(0, 3 * (nx - 1), collect, 0)
    for m, out in enumerate((og, ou, od)):
        out[0] = acc[m]

    returned(jnp.int32(ny - 1), 0)

    total = ny * group
    lane = lax.broadcasted_iota(jnp.int32, (1, total), 1)
    lane_q = fifth(lane)
    wanted = slot_id(lane_q // nz, lane_q & (nz - 1), lane - CAP * lane_q)
    pick = [jnp.where(col_target[k] == wanted, 1.0, 0.0) for k in range(2)]
    both = (pick[0] + pick[1]).astype(BF16)
    pick = [p.astype(BF16) for p in pick]
    sums = [jnp.zeros((rows, 1), F32) for _ in range(2)]
    for c in range(chunks):
        cols = slice(c * LANES, (c + 1) * LANES)
        out = [jnp.dot(p, back[0, c], preferred_element_type=F32) for p in pick]
        mixed[:, cols] = (pr[0] * out[0] + pr[1] * out[1]).astype(BF16)
        gtok[:, cols] = jnp.dot(both, back[1, c], preferred_element_type=F32).astype(BF16)
        cot_c = cot[:, cols].astype(F32)
        sums = [s + jnp.sum(cot_c * o, axis=1, keepdims=True) for s, o in zip(sums, out)]
    for k in range(2):
        gprob[:, k:k + 1] = sums[k]

    count = ny * nz
    for buf, sem in ((send, fs_sem), (rsend, rs_sem)):
        rest = buf.at[pl.ds(1, count - 1)]
        remote(rest, rest, sem, fr_sem.at[0], twin).wait_send()
    for dx in range(nx):
        remote(mine, mine, wcs_sem.at[dx], wcr_sem.at[dx], twin).wait_send()
        if dx:
            remote(mine, mine, wxs_sem.at[dx], wxr_sem.at[dx], at_x(dx)).wait_send()


def per_device(nx, nz_lo, nz_hi, tokens, cotangent, gate_probs, expert_ids, gate_weight, up_weight, down_weight):
    rows, width = tokens.shape
    wide_n = gate_weight.shape[2]
    shard = gate_weight.shape[1]
    experts = nz_lo * nz_hi * NY
    chunks = width // LANES
    tall = 2 * chunks
    slots = experts * CAP
    message = (experts, CAP * tall, LANES)
    vmem = pl.BlockSpec(memory_space=pltpu.VMEM)
    anywhere = pl.BlockSpec(memory_space=pl.ANY)
    dma = pltpu.SemaphoreType.DMA
    grad = jax.ShapeDtypeStruct((1, shard, wide_n), F32)
    pieces = (3 * nx, shard, wide_n)
    return pl.pallas_call(
        functools.partial(kernel, nx, nz_lo, nz_hi, NY),
        out_shape=(
            jax.ShapeDtypeStruct((rows, width), BF16),
            jax.ShapeDtypeStruct((rows, width), BF16),
            jax.ShapeDtypeStruct((rows, 2), F32),
            grad, grad, grad,
        ),
        in_specs=[vmem] * 4 + [anywhere] * 3,
        out_specs=(vmem,) * 6,
        scratch_shapes=[
            pltpu.VMEM((3, 2 * nx, shard, wide_n), BF16),
            pltpu.VMEM(message, BF16),
            pltpu.VMEM(message, BF16),
            pltpu.VMEM(message, BF16),
            pltpu.VMEM(message, BF16),
            pltpu.VMEM((slots // NY * tall, LANES), F32),
            pltpu.VMEM((2, chunks, slots, LANES), BF16),
            pltpu.VMEM((3, slots, wide_n), BF16),
            pltpu.VMEM((2 * rows, width), BF16),
            pltpu.VMEM(pieces, BF16),
            pltpu.VMEM(pieces, BF16),
            pltpu.VMEM(pieces, BF16),
            pltpu.VMEM(pieces, BF16),
            pltpu.VMEM((3, shard, wide_n), F32),
            pltpu.VMEM((2, chunks, slots, LANES), BF16),
            dma((3,)), dma, dma((NY,)), dma, dma((NY,)),
            dma((nx,)), dma((nx,)), dma((nx,)), dma((nx,)),
            dma((3 * nx,)), dma((3 * nx,)), dma((3 * nx,)), dma((3 * nx,)),
        ],
        compiler_params=pltpu.CompilerParams(
            collective_id=0, has_side_effects=True, vmem_limit_bytes=56 * 2**20
        ),
    )(tokens, cotangent, gate_probs, expert_ids, gate_weight, up_weight, down_weight)


def solution(mesh):
    tokens = P(("dp", "expouter", "expinner"), None)
    weights = P(("expouter", "expinner"), "dp", None)
    nx = mesh.shape["dp"] // 2
    nz_lo = mesh.shape["expouter"]
    nz_hi = mesh.shape["expinner"] // NY
    return jax.shard_map(
        functools.partial(per_device, nx, nz_lo, nz_hi),
        mesh=mesh,
        in_specs=(tokens,) * 4 + (weights,) * 3,
        out_specs=(tokens,) * 3 + (weights,) * 3,
        check_vma=False,
    )
```

time: 330 us -> 148 us (0.45)
  waiting for transfers between devices: 201 us -> 0 us
  Pallas kernels: 0 us -> 136 us
  starting transfers between devices: 55.7 us -> 0 us
  matrix products: 28 us -> 0 us
  between operations: 14.4 us -> 0.66 us
  local copies, waits for them, and re-layouts: 22.6 us -> 9.13 us
  other arithmetic: 7.8 us -> 0 us
    all_to_all x6 -> x0, waiting for transfers between devices: 198 us -> none  [the longest x1 51.8 us: per_device(): lax.all_to_all(shaped[1], ('expouter', 'expinner'), split_axis=0, concat_...]
    pallas_call x0 -> x1, Pallas kernels: none -> 136 us  [per_device(): pl.pallas_call(functools.partial(kernel, nx, nz_lo, nz_hi, NY), out_shape...]
    all_to_all x6 -> x0, starting transfers between devices: 55.5 us -> none  [the longest x1 19.4 us: per_device(): lax.all_to_all(shaped[0], ('expouter', 'expinner'), split_axis=0, concat_...]
    dot_general x11 -> x0, matrix products: 28 us -> none  [the longest x3 10.8 us: contract_rows(): lax.dot_general(left, right, (((0,), (0,)), ((), ())), preferred_element_...]
    reshape x9 -> x0, local copies, waits for them, and re-layouts: 9.14 us -> none  [the longest x1 2.15 us: per_device(): expert_out.reshape(expert_count, capacity, model_width)]
    all_to_all x4 -> x0, local copies, waits for them, and re-layouts: 7.26 us -> none  [the longest x2 3.64 us: per_device(): lax.all_to_all(rows_o, 'dp', split_axis=1, concat_axis=0, tiled=True)]
    unnamed x15 -> x17, local copies, waits for them, and re-layouts: 1.56 us -> 7.61 us
    reduce_sum x4 -> x0, other arithmetic: 5.95 us -> none  [the longest x1 3.62 us: per_device(): jnp.sum(cotangent[:, None, :].astype(jnp.float32) * pick_float, axis=2)]
  transfers between devices with their start and end apart: 12 -> 0, of which waited for: 5 -> 0; matrix products, arithmetic and copies ran while one was open for 14% -> 0% of each run, Pallas kernels for 0% -> 0%
where the time goes in v2:
time: 148 us; the launch traced here: 146 us
  Pallas kernels  136 us (92%)
  local copies, waits for them, and re-layouts  9.13 us (6%)
    pallas_call x1, Pallas kernels, per_device(): pl.pallas_call(functools.partial(kernel, nx, nz_lo, nz_hi, NY), out_shape...  136 us
    unnamed x17, local copies, waits for them, and re-layouts  7.61 us

profile of v2, /device:TPU:1, one launch (start us, length us, event | category | flops | bytes accessed | tf_op | source)
XLA Modules:
  0.0 146.1 jit_solution(486543863531942673)
XLA Ops:
  0.6 0.0 copy-start.4
  0.6 1.4 copy.13.probs
  2.1 0.0 copy-done.4
  2.1 0.7 copy.14.ids
  2.8 136.3 %shard_map.118 = (bf16[128,1024]{1,0:T(8,128)(2,1)}, bf16[128,1024]{1,0:T(8,128)(2,1)}, f32[128,2]{1,0:T(8,128)}, f32[1,128,768]{2,1,0:T(8,128)}, f32[1,128,768]{2,1,0:T(8,128)}, /*index=5*/f32[1,128,768]{2,1,0:T(8,128)}) custom-call(bf16[128,1024]{1,0:T(8,128)(2,1)} %tok.1, bf16[128,1024]{1,0:T(8,128)(2,1)} %cot.1, f32[128,2]{1,0:T(8,128)} %copy.13.probs, ...), custom_call_target="tpu_custom_call" | custom-call | tf_op jit(solution)/shard_map/pallas_call | solution.py:304
  139.1 0.0 copy-start.3
  139.1 1.5 %copy.15 = f32[128,2]{0,1:T(2,128)} copy(f32[128,2]{1,0:T(8,128)} %get-tuple-element.8) | data formatting | bytes 2048 | tf_op jit(solution)/shard_map/pallas_call | solution.py:304
  140.6 0.0 copy-start.2
  140.6 1.7 %copy.21 = bf16[128,1024]{1,0:T(8,128)(2,1)} copy(bf16[128,1024]{1,0:T(8,128)(2,1)} %get-tuple-element.18) | data formatting | bytes 524288
  142.3 0.0 copy-done.3
  142.3 0.7 copy.22
  143.0 0.0 copy-done.2
  143.0 0.0 copy-start.1
  143.0 0.7 copy.23
  143.8 0.4 copy-done.1
  144.2 0.0 copy-start
  144.2 0.7 copy.24
  144.9 0.4 copy-done
  145.3 0.7 copy.25
Async XLA Ops:
  0.6 1.4 copy-start.4
  139.1 3.3 %copy-start.3 = (bf16[128,1024]{1,0:T(8,128)(2,1)S(1)}, bf16[128,1024]{1,0:T(8,128)(2,1)}, u32[]{:S(2)}) copy-start(bf16[128,1024]{1,0:T(8,128)(2,1)} %get-tuple-element.19) | copy-start | bytes 786436
  140.6 2.4 %copy-start.2 = (f32[1,128,768]{2,1,0:T(8,128)S(1)}, f32[1,128,768]{2,1,0:T(8,128)}, u32[]{:S(2)}) copy-start(f32[1,128,768]{2,1,0:T(8,128)} %get-tuple-element.21) | copy-start | bytes 1179652
  143.0 1.1 copy-start.1
  144.2 1.1 copy-start

commit v3 on v2

--- a/solution.py
+++ b/solution.py
@@ -21,16 +21,16 @@
 
 def kernel(
     nx, nz_lo, nz_hi, ny,
-    tok, cot, probs, ids, wg, wu, wd,
+    tok_in, cot_in, probs, ids, wg, wu, wd,
     mixed, gtok, gprob, og, ou, od,
-    weights, send, recv, rsend, rrecv, wide, xo, acts, scaled,
+    tok, cot, picked, weights, send, recv, rsend, rrecv, wide, xo, acts, scaled,
     csend, crecv, xsend, xrecv, acc, back,
-    load_sem, fs_sem, fr_sem, rs_sem, rr_sem,
+    load_sem, store_sem, fs_sem, fr_sem, rs_sem, rr_sem,
     wxs_sem, wxr_sem, wcs_sem, wcr_sem,
     gcs_sem, gcr_sem, gxs_sem, gxr_sem,
 ):
     nz = nz_lo * nz_hi
-    width = tok.shape[1]
+    rows, width = tok.shape
     chunks = width // LANES
     tall = 2 * chunks
     group = nz * CAP
@@ -57,8 +57,14 @@
             device_id=device, device_id_type=MESH,
         )
 
-    own = [pltpu.make_async_copy(w.at[0], weights.at[m, me], load_sem.at[m]) for m, w in enumerate((wg, wu, wd))]
-    for copy in own:
+    loads = [
+        pltpu.make_async_copy(a, b, load_sem.at[i])
+        for i, (a, b) in enumerate(
+            [(tok_in, tok), (cot_in, cot)]
+            + [(w.at[0], weights.at[m, me]) for m, w in enumerate((wg, wu, wd))]
+        )
+    ]
+    for copy in loads:
         copy.start()
     barrier = pltpu.get_barrier_semaphore()
 
@@ -71,19 +77,20 @@
         pl.semaphore_signal(barrier, inc=1, device_id=at_x(dx), device_id_type=MESH)
     pl.semaphore_signal(barrier, inc=1, device_id=twin, device_id_type=MESH)
 
-    rows = tok.shape[0]
     idf = ids[...].astype(F32)
-    down_id = [jnp.broadcast_to(idf[:, k:k + 1], (rows, rows)) for k in range(2)]
-    over_id = [jnp.transpose(b) for b in down_id]
+    over_id = [jnp.broadcast_to(idf[k:k + 1, :], (rows, rows)) for k in range(2)]
+    down_id = [jnp.transpose(b) for b in over_id]
     first = lax.broadcasted_iota(jnp.int32, (rows, rows), 0)
     second = lax.broadcasted_iota(jnp.int32, (rows, rows), 1)
     col_target, row_target = [], []
     for k in range(2):
         hits = sum(jnp.where((down_id[k] == over_id[j]) & (second < first), 1.0, 0.0) for j in range(2))
-        col_target.append(idf[:, k:k + 1] * CAP + jnp.sum(hits, axis=1, keepdims=True))
+        col_target.append(down_id[k][:, 0:1] * CAP + jnp.sum(hits, axis=1, keepdims=True))
         hits = sum(jnp.where((down_id[j] == over_id[k]) & (first < second), 1.0, 0.0) for j in range(2))
-        row_target.append(over_id[k][0:1, :] * CAP + jnp.sum(hits, axis=0, keepdims=True))
-    pr = [probs[:, k:k + 1] for k in range(2)]
+        row_target.append(idf[k:k + 1, :] * CAP + jnp.sum(hits, axis=0, keepdims=True))
+    pr = [jnp.transpose(jnp.broadcast_to(probs[k:k + 1, :], (rows, rows)))[:, 0:1] for k in range(2)]
+    for copy in loads[:2]:
+        copy.wait()
     for k in range(2):
         scaled[k * rows:(k + 1) * rows, :] = (pr[k] * cot[...].astype(F32)).astype(BF16)
 
@@ -111,7 +118,9 @@
         send[pl.ds(dy * nz, nz)] = wide[...].astype(BF16).reshape(nz, CAP * tall, LANES)
 
     def scatter(dy, src, dst, ss, rs, sign):
-        def one(dz, _):
+        def one(n, _):
+            j = nz - 1 - n
+            dz = jnp.where(lax.rem(j, 2) == 1, (j + 1) // 2, lax.rem(nz - j // 2, nz))
             i = dy * nz + dz
 
             @pl.when(i > 0)
@@ -127,16 +136,15 @@
             pltpu.make_async_copy(src.at[0], dst.at[0], rs.at[0]).start()
 
     pack(jnp.int32(0))
-    for copy in own:
+    for copy in loads[2:]:
         copy.wait()
     pl.semaphore_wait(barrier, ny * nz - 1 + nx - 1 + 1)
+    scatter(jnp.int32(0), send, recv, fs_sem, fr_sem, 1)
 
     mine = weights.at[:, me]
     remote(mine, mine, wcs_sem.at[0], wcr_sem.at[0], twin).start()
     for dx in range(1, nx):
         remote(mine, mine, wxs_sem.at[dx], wxr_sem.at[dx], at_x(dx)).start()
-
-    scatter(jnp.int32(0), send, recv, fs_sem, fr_sem, 1)
 
     def pack_and_send(dy, _):
         pack(dy)
@@ -247,6 +255,23 @@
 
     lax.fori_loop(0, ny - 1, returned, 0)
 
+    early = (ny - 1) * group
+
+    def chosen(start, count):
+        lane = lax.broadcasted_iota(jnp.int32, (1, count), 1) + start
+        lane_q = fifth(lane)
+        wanted = slot_id(lane_q // nz, lane_q & (nz - 1), lane - CAP * lane_q)
+        pick = [jnp.where(col_target[k] == wanted, 1.0, 0.0) for k in range(2)]
+        return [p.astype(BF16) for p in (pick[0], pick[1], pick[0] + pick[1])]
+
+    def gather(pick, here, c):
+        return [jnp.dot(p, back[part, c, here, :], preferred_element_type=F32) for p, part in zip(pick, (0, 0, 1))]
+
+    pick = chosen(0, early)
+    for c in range(chunks):
+        for k, value in enumerate(gather(pick, slice(0, early), c)):
+            picked[k, :, c * LANES:(c + 1) * LANES] = value
+
     def collect(i, _):
         remote(xsend.at[i], xrecv.at[i], gxs_sem.at[i], gxr_sem.at[i], at_x(lax.rem(i // 3 + 1, nx))).wait()
         m = lax.rem(i, 3)
@@ -254,28 +279,25 @@
         return 0
 
     lax.fori_loop(0, 3 * (nx - 1), collect, 0)
-    for m, out in enumerate((og, ou, od)):
-        out[0] = acc[m]
+    stores = [pltpu.make_async_copy(acc.at[m], out.at[0], store_sem.at[m]) for m, out in enumerate((og, ou, od))]
+    for copy in stores:
+        copy.start()
 
     returned(jnp.int32(ny - 1), 0)
-
-    total = ny * group
-    lane = lax.broadcasted_iota(jnp.int32, (1, total), 1)
-    lane_q = fifth(lane)
-    wanted = slot_id(lane_q // nz, lane_q & (nz - 1), lane - CAP * lane_q)
-    pick = [jnp.where(col_target[k] == wanted, 1.0, 0.0) for k in range(2)]
-    both = (pick[0] + pick[1]).astype(BF16)
-    pick = [p.astype(BF16) for p in pick]
+    pick = chosen(early, group)
     sums = [jnp.zeros((rows, 1), F32) for _ in range(2)]
     for c in range(chunks):
         cols = slice(c * LANES, (c + 1) * LANES)
-        out = [jnp.dot(p, back[0, c], preferred_element_type=F32) for p in pick]
+        out = [picked[k, :, cols] + value for k, value in enumerate(gather(pick, slice(early, early + group), c))]
         mixed[:, cols] = (pr[0] * out[0] + pr[1] * out[1]).astype(BF16)
-        gtok[:, cols] = jnp.dot(both, back[1, c], preferred_element_type=F32).astype(BF16)
+        gtok[:, cols] = out[2].astype(BF16)
         cot_c = cot[:, cols].astype(F32)
         sums = [s + jnp.sum(cot_c * o, axis=1, keepdims=True) for s, o in zip(sums, out)]
     for k in range(2):
-        gprob[:, k:k + 1] = sums[k]
+        gprob[k:k + 1, :] = jnp.transpose(jnp.broadcast_to(sums[k], (rows, rows)))[0:1, :]
+
+    for copy in stores:
+        copy.wait()
 
     count = ny * nz
     for buf, sem in ((send, fs_sem), (rsend, rs_sem)):
@@ -285,6 +307,20 @@
         remote(mine, mine, wcs_sem.at[dx], wcr_sem.at[dx], twin).wait_send()
         if dx:
             remote(mine, mine, wxs_sem.at[dx], wxr_sem.at[dx], at_x(dx)).wait_send()
+
+
+def hand_over(*refs):
+    count = len(refs) // 3
+    sems = refs[-1]
+    into = [pltpu.make_async_copy(refs[i], refs[2 * count + i], sems.at[0, i]) for i in range(count)]
+    out = [pltpu.make_async_copy(refs[2 * count + i], refs[count + i], sems.at[1, i]) for i in range(count)]
+    for copy in into:
+        copy.start()
+    for first, second in zip(into, out):
+        first.wait()
+        second.start()
+    for copy in out:
+        copy.wait()
 
 
 def per_device(nx, nz_lo, nz_hi, tokens, cotangent, gate_probs, expert_ids, gate_weight, up_weight, down_weight):
@@ -301,17 +337,21 @@
     dma = pltpu.SemaphoreType.DMA
     grad = jax.ShapeDtypeStruct((1, shard, wide_n), F32)
     pieces = (3 * nx, shard, wide_n)
-    return pl.pallas_call(
+    shapes = (
+        jax.ShapeDtypeStruct((rows, width), BF16),
+        jax.ShapeDtypeStruct((rows, width), BF16),
+        jax.ShapeDtypeStruct((2, rows), F32),
+        grad, grad, grad,
+    )
+    results = pl.pallas_call(
         functools.partial(kernel, nx, nz_lo, nz_hi, NY),
-        out_shape=(
-            jax.ShapeDtypeStruct((rows, width), BF16),
-            jax.ShapeDtypeStruct((rows, width), BF16),
-            jax.ShapeDtypeStruct((rows, 2), F32),
-            grad, grad, grad,
-        ),
-        in_specs=[vmem] * 4 + [anywhere] * 3,
-        out_specs=(vmem,) * 6,
+        out_shape=shapes,
+        in_specs=[anywhere] * 2 + [vmem] * 2 + [anywhere] * 3,
+        out_specs=(vmem,) * 3 + (anywhere,) * 3,
         scratch_shapes=[
+            pltpu.VMEM((rows, width), BF16),
+            pltpu.VMEM((rows, width), BF16),
+            pltpu.VMEM((3, rows, width), F32),
             pltpu.VMEM((3, 2 * nx, shard, wide_n), BF16),
             pltpu.VMEM(message, BF16),
             pltpu.VMEM(message, BF16),
@@ -327,14 +367,22 @@
             pltpu.VMEM(pieces, BF16),
             pltpu.VMEM((3, shard, wide_n), F32),
             pltpu.VMEM((2, chunks, slots, LANES), BF16),
-            dma((3,)), dma, dma((NY,)), dma, dma((NY,)),
+            dma((5,)), dma((3,)), dma, dma((NY,)), dma, dma((NY,)),
             dma((nx,)), dma((nx,)), dma((nx,)), dma((nx,)),
             dma((3 * nx,)), dma((3 * nx,)), dma((3 * nx,)), dma((3 * nx,)),
         ],
         compiler_params=pltpu.CompilerParams(
             collective_id=0, has_side_effects=True, vmem_limit_bytes=56 * 2**20
         ),
-    )(tokens, cotangent, gate_probs, expert_ids, gate_weight, up_weight, down_weight)
+    )(tokens, cotangent, gate_probs.T, expert_ids.T, gate_weight, up_weight, down_weight)
+    mixed, gtok, gprob, *grads = pl.pallas_call(
+        hand_over,
+        out_shape=shapes,
+        in_specs=[anywhere] * 6,
+        out_specs=(anywhere,) * 6,
+        scratch_shapes=[pltpu.VMEM(a.shape, a.dtype) for a in shapes] + [dma((2, 6))],
+    )(*results)
+    return (mixed, gtok, gprob.T, *grads)
 
 
 def solution(mesh):

time: 148 us -> 139 us (0.939); the launches traced: 146 us -> 139 us
  local copies, waits for them, and re-layouts: 9.13 us -> 0 us
  Pallas kernels: 136 us -> 138 us
    unnamed x17 -> x0, local copies, waits for them, and re-layouts: 7.61 us -> none
    pallas_call x0 -> x1, Pallas kernels: none -> 2.27 us  [per_device(): pl.pallas_call(hand_over, out_shape=shapes, in_specs=[anywhere] * 6, out_...]
    pallas_call x1 -> x0, local copies, waits for them, and re-layouts: 1.52 us -> none  [per_device(): pl.pallas_call(functools.partial(kernel, nx, nz_lo, nz_hi, NY), out_shape...]
where the time goes in v3:
time: 139 us
  Pallas kernels  138 us (99%)
    pallas_call x1, Pallas kernels, per_device(): pl.pallas_call(functools.partial(kernel, nx, nz_lo, nz_hi, NY), out_shape...  136 us

profile of v3, /device:TPU:1, one launch (start us, length us, event | category | flops | bytes accessed | tf_op | source)
XLA Modules:
  0.0 138.6 jit_solution(11607957140029960154)
XLA Ops:
  0.6 135.7 %shard_map.118 = (bf16[128,1024]{1,0:T(8,128)(2,1)}, bf16[128,1024]{1,0:T(8,128)(2,1)}, f32[2,128]{1,0:T(2,128)}, f32[1,128,768]{2,1,0:T(8,128)}, f32[1,128,768]{2,1,0:T(8,128)}, /*index=5*/f32[1,128,768]{2,1,0:T(8,128)}) custom-call(bf16[128,1024]{1,0:T(8,128)(2,1)} %tok_in.1, bf16[128,1024]{1,0:T(8,128)(2,1)} %cot_in.1, f32[2,128]{1,0:T(2,128)} %bitcast.3, ...), custom_call_target="tpu_custom_call" | custom-call | tf_op jit(solution)/shard_map/pallas_call | solution.py:346
  136.3 2.3 %shard_map.119 = (bf16[128,1024]{1,0:T(8,128)(2,1)}, bf16[128,1024]{1,0:T(8,128)(2,1)}, f32[2,128]{1,0:T(2,128)}, f32[1,128,768]{2,1,0:T(8,128)}, f32[1,128,768]{2,1,0:T(8,128)}, /*index=5*/f32[1,128,768]{2,1,0:T(8,128)}) custom-call(bf16[128,1024]{1,0:T(8,128)(2,1)} %get-tuple-element.18.refs_0_, bf16[128,1024]{1,0:T(8,128)(2,1)} %get-tuple-element.19.refs_1_, ...), custom_call_target="tpu_custom_call" | custom-call | tf_op jit(solution)/shard_map/pallas_call | solution.py:378

commit v4 on v3

--- a/solution.py
+++ b/solution.py
@@ -121,6 +121,8 @@
         def one(n, _):
             j = nz - 1 - n
             dz = jnp.where(lax.rem(j, 2) == 1, (j + 1) // 2, lax.rem(nz - j // 2, nz))
+            if sign < 0:
+                dz = lax.rem(z - n + nz, nz)
             i = dy * nz + dz
 
             @pl.when(i > 0)

time: 139 us -> 135 us (0.971)
  the two profiles are of different devices: /device:TPU:1 before, /device:TPU:199 now
where the time goes in v4:
time: 135 us
  Pallas kernels  134 us (99%)
    pallas_call x1, Pallas kernels, per_device(): pl.pallas_call(functools.partial(kernel, nx, nz_lo, nz_hi, NY), out_shape...  132 us

profile of v4, /device:TPU:199, one launch (start us, length us, event | category | flops | bytes accessed | tf_op | source)
XLA Modules:
  0.0 135.1 jit_solution(17228214954630881630)
XLA Ops:
  0.6 132.1 %shard_map.118 = (bf16[128,1024]{1,0:T(8,128)(2,1)}, bf16[128,1024]{1,0:T(8,128)(2,1)}, f32[2,128]{1,0:T(2,128)}, f32[1,128,768]{2,1,0:T(8,128)}, f32[1,128,768]{2,1,0:T(8,128)}, /*index=5*/f32[1,128,768]{2,1,0:T(8,128)}) custom-call(bf16[128,1024]{1,0:T(8,128)(2,1)} %tok_in.1, bf16[128,1024]{1,0:T(8,128)(2,1)} %cot_in.1, f32[2,128]{1,0:T(2,128)} %bitcast.3, ...), custom_call_target="tpu_custom_call" | custom-call | tf_op jit(solution)/shard_map/pallas_call | solution.py:348
  132.8 2.3 %shard_map.119 = (bf16[128,1024]{1,0:T(8,128)(2,1)}, bf16[128,1024]{1,0:T(8,128)(2,1)}, f32[2,128]{1,0:T(2,128)}, f32[1,128,768]{2,1,0:T(8,128)}, f32[1,128,768]{2,1,0:T(8,128)}, /*index=5*/f32[1,128,768]{2,1,0:T(8,128)}) custom-call(bf16[128,1024]{1,0:T(8,128)(2,1)} %get-tuple-element.18.refs_0_, bf16[128,1024]{1,0:T(8,128)(2,1)} %get-tuple-element.19.refs_1_, ...), custom_call_target="tpu_custom_call" | custom-call | tf_op jit(solution)/shard_map/pallas_call | solution.py:380

commit v5 on v4

--- a/solution.py
+++ b/solution.py
@@ -68,11 +68,13 @@
         copy.start()
     barrier = pltpu.get_barrier_semaphore()
 
-    def greet(i, _):
-        pl.semaphore_signal(barrier, inc=1, device_id=at_yz(i // nz, lax.rem(i, nz)), device_id_type=MESH)
-        return 0
-
-    lax.fori_loop(1, ny * nz, greet, 0)
+    for dz in sorted(range(nz), key=lambda d: -min(d, nz - d)):
+        for dy in range(ny):
+            if dy or dz:
+                tz = (z + dz) & (nz - 1)
+                ty = (y + dy) & (ny - 1)
+                there = {"expouter": tz & (nz_lo - 1), "expinner": (tz // nz_lo) * ny + ty}
+                pl.semaphore_signal(barrier, inc=1, device_id=there, device_id_type=MESH)
     for dx in range(1, nx):
         pl.semaphore_signal(barrier, inc=1, device_id=at_x(dx), device_id_type=MESH)
     pl.semaphore_signal(barrier, inc=1, device_id=twin, device_id_type=MESH)

time: 135 us -> 135 us (level)
  the two profiles are of different devices: /device:TPU:199 before, /device:TPU:193 now
where the time goes in v5:
time: 135 us; the launch traced here: 134 us
  Pallas kernels  134 us (99%)
    pallas_call x1, Pallas kernels, per_device(): pl.pallas_call(functools.partial(kernel, nx, nz_lo, nz_hi, NY), out_shape...  131 us

profile of v5, /device:TPU:193, one launch (start us, length us, event | category | flops | bytes accessed | tf_op | source)
XLA Modules:
  0.0 134.3 jit_solution(2185955212503892071)
XLA Ops:
  0.6 131.4 %shard_map.118 = (bf16[128,1024]{1,0:T(8,128)(2,1)}, bf16[128,1024]{1,0:T(8,128)(2,1)}, f32[2,128]{1,0:T(2,128)}, f32[1,128,768]{2,1,0:T(8,128)}, f32[1,128,768]{2,1,0:T(8,128)}, /*index=5*/f32[1,128,768]{2,1,0:T(8,128)}) custom-call(bf16[128,1024]{1,0:T(8,128)(2,1)} %tok_in.1, bf16[128,1024]{1,0:T(8,128)(2,1)} %cot_in.1, f32[2,128]{1,0:T(2,128)} %bitcast.3, ...), custom_call_target="tpu_custom_call" | custom-call | tf_op jit(solution)/shard_map/pallas_call | solution.py:350
  132.1 2.3 %shard_map.119 = (bf16[128,1024]{1,0:T(8,128)(2,1)}, bf16[128,1024]{1,0:T(8,128)(2,1)}, f32[2,128]{1,0:T(2,128)}, f32[1,128,768]{2,1,0:T(8,128)}, f32[1,128,768]{2,1,0:T(8,128)}, /*index=5*/f32[1,128,768]{2,1,0:T(8,128)}) custom-call(bf16[128,1024]{1,0:T(8,128)(2,1)} %get-tuple-element.18.refs_0_, bf16[128,1024]{1,0:T(8,128)(2,1)} %get-tuple-element.19.refs_1_, ...), custom_call_target="tpu_custom_call" | custom-call | tf_op jit(solution)/shard_map/pallas_call | solution.py:382

commit v6 on v5

--- a/solution.py
+++ b/solution.py
@@ -64,8 +64,6 @@
             + [(w.at[0], weights.at[m, me]) for m, w in enumerate((wg, wu, wd))]
         )
     ]
-    for copy in loads:
-        copy.start()
     barrier = pltpu.get_barrier_semaphore()
 
     for dz in sorted(range(nz), key=lambda d: -min(d, nz - d)):
@@ -78,6 +76,8 @@
     for dx in range(1, nx):
         pl.semaphore_signal(barrier, inc=1, device_id=at_x(dx), device_id_type=MESH)
     pl.semaphore_signal(barrier, inc=1, device_id=twin, device_id_type=MESH)
+    for copy in loads:
+        copy.start()
 
     idf = ids[...].astype(F32)
     over_id = [jnp.broadcast_to(idf[k:k + 1, :], (rows, rows)) for k in range(2)]
@@ -287,12 +287,19 @@
     for copy in stores:
         copy.start()
 
-    returned(jnp.int32(ny - 1), 0)
+    last = pl.ds((ny - 1) * nz, nz)
+    remote(rrecv.at[last], rrecv.at[last], rs_sem, rr_sem.at[ny - 1], twin).wait_recv()
+    wide[...] = rrecv[last].reshape(nz * CAP * tall, LANES).astype(F32)
     pick = chosen(early, group)
+    stacked = jnp.concatenate(pick[:2], axis=0)
     sums = [jnp.zeros((rows, 1), F32) for _ in range(2)]
     for c in range(chunks):
         cols = slice(c * LANES, (c + 1) * LANES)
-        out = [picked[k, :, cols] + value for k, value in enumerate(gather(pick, slice(early, early + group), c))]
+        out_rows = wide[pl.ds(c, group, stride=tall), :].astype(BF16)
+        grad_rows = wide[pl.ds(chunks + c, group, stride=tall), :].astype(BF16)
+        pair = jnp.dot(stacked, out_rows, preferred_element_type=F32)
+        out = [picked[k, :, cols] + pair[k * rows:(k + 1) * rows] for k in range(2)]
+        out.append(picked[2, :, cols] + jnp.dot(pick[2], grad_rows, preferred_element_type=F32))
         mixed[:, cols] = (pr[0] * out[0] + pr[1] * out[1]).astype(BF16)
         gtok[:, cols] = out[2].astype(BF16)
         cot_c = cot[:, cols].astype(F32)

time: 135 us -> 135 us (level)
  the two profiles are of different devices: /device:TPU:193 before, /device:TPU:199 now
where the time goes in v6:
time: 135 us; the launch traced here: 134 us
  Pallas kernels  134 us (99%)
    pallas_call x1, Pallas kernels, per_device(): pl.pallas_call(functools.partial(kernel, nx, nz_lo, nz_hi, NY), out_shape...  131 us

profile of v6, /device:TPU:199, one launch (start us, length us, event | category | flops | bytes accessed | tf_op | source)
XLA Modules:
  0.0 134.3 jit_solution(763505251196863044)
XLA Ops:
  0.6 131.4 %shard_map.118 = (bf16[128,1024]{1,0:T(8,128)(2,1)}, bf16[128,1024]{1,0:T(8,128)(2,1)}, f32[2,128]{1,0:T(2,128)}, f32[1,128,768]{2,1,0:T(8,128)}, f32[1,128,768]{2,1,0:T(8,128)}, /*index=5*/f32[1,128,768]{2,1,0:T(8,128)}) custom-call(bf16[128,1024]{1,0:T(8,128)(2,1)} %tok_in.1, bf16[128,1024]{1,0:T(8,128)(2,1)} %cot_in.1, f32[2,128]{1,0:T(2,128)} %bitcast.3, ...), custom_call_target="tpu_custom_call" | custom-call | tf_op jit(solution)/shard_map/pallas_call | solution.py:357
  132.0 2.3 %shard_map.119 = (bf16[128,1024]{1,0:T(8,128)(2,1)}, bf16[128,1024]{1,0:T(8,128)(2,1)}, f32[2,128]{1,0:T(2,128)}, f32[1,128,768]{2,1,0:T(8,128)}, f32[1,128,768]{2,1,0:T(8,128)}, /*index=5*/f32[1,128,768]{2,1,0:T(8,128)}) custom-call(bf16[128,1024]{1,0:T(8,128)(2,1)} %get-tuple-element.18.refs_0_, bf16[128,1024]{1,0:T(8,128)(2,1)} %get-tuple-element.19.refs_1_, ...), custom_call_target="tpu_custom_call" | custom-call | tf_op jit(solution)/shard_map/pallas_call | solution.py:389
